TPU v7x, 32 devices: a whole 2x2x4 slice. The times are simulated.
32 devices in a mesh: mem: 4 (over y, x), dom: 8 (over z, core).
Axes of the slice: x: 2, y: 2, z: 4, core: 2. Of those that a mesh axis runs over, the one named last changes fastest.
Arguments:
- sample_vectors_prior: float32 [16, 5, 256, 256], P('mem', None, 'dom'), may hold values from -6 to 6
- smoothing_number: float32 [5, 256, 256], P(None, 'dom'), may hold values from 0.02 to 0.2
- cross_quantity_factor: float32 [5, 5], replicated, may hold values from -0.6 to 0.6
- obs_tile: int32 [2, 2048, 1], replicated, may hold values from 0 to 7; in each aligned block of 2048 rows (0 to 2047, 2048 to 4095, ..., all dimensions but the last counted through in order) at most 512 rows name the same one
- measured_gridpoint: int32 [2, 2048], replicated, may hold values from 0 to 7904
- obs_field: int32 [2, 2048], replicated, may hold values from 0 to 4
- obs_weights: float32 [2, 2048, 4], replicated, may hold values from 0.1 to 0.5
- obs_values: float32 [2, 2048], replicated, may hold values from -8 to 8
- observation_variance: float32 [2, 2048], replicated, may hold values from 0.2 to 2
- localization: float32 [2, 8, 2048], P(None, 'dom'), may hold values from 0.001 to 0.02
Outputs:
- analysis: float32 [16, 5, 256, 256], P('mem', None, 'dom')
Inputs may be any that keep to these rules, and one draw needn't show every extreme that they name: `obs_tile`: in each batch at most 512 observations share an owning tile, and in some batch some tile owns exactly 512. Local row measured_gridpoint // 255, column measured_gridpoint % 255; the four points used lie in the owning tile.
All inputs are finite; a program needn't handle non-finite values.
Results may differ from a plain program's by a relative error of at most 0.0001.
Values sent between devices are 32-bit elements; how exact they have to be, the bound alone decides.
A program may use at most 128 MiB of HBM per device.

v0:
```python
import jax
import jax.numpy as jnp
from jax import lax
from jax.sharding import PartitionSpec as P

STEPS = 2


def with_halo(cells, sides, width):
    for axis, dim in sides:
        count = lax.axis_size(axis)
        ends = count - 1
        head = lax.slice_in_dim(cells, 0, width, axis=dim)
        tail = lax.slice_in_dim(cells, cells.shape[dim] - width, cells.shape[dim], axis=dim)
        cells = jnp.concatenate(
            [
                lax.ppermute(tail, axis, [(i, (i + 1) % count) for i in range(ends)]),
                cells,
                lax.ppermute(head, axis, [((i + 1) % count, i) for i in range(ends)]),
            ],
            axis=dim,
        )
    return cells


def predicted_quantity(sample_vectors_prior, smoothing_number, cross_quantity_factor):
    padded = with_halo(sample_vectors_prior, (("dom", 2),), 1)
    padded = jnp.pad(padded, ((0, 0), (0, 0), (0, 0), (1, 1)))
    lap = padded[:, :, 2:, 1:-1] + padded[:, :, :-2, 1:-1]
    lap = lap + padded[:, :, 1:-1, 2:] + padded[:, :, 1:-1, :-2] - 4.0 * sample_vectors_prior
    mixed = jnp.einsum(
        "fg,mgxy->mfxy",
        cross_quantity_factor,
        sample_vectors_prior,
        precision=lax.Precision.HIGHEST,
    )
    return sample_vectors_prior + smoothing_number[None] * lap + mixed


def local_priors(
    sample_vectors_prior, obs_tile, measured_gridpoint, obs_field, obs_weights, batch_index, my_tile
):
    sample_total_size, fields, tile_row_count, columns = sample_vectors_prior.shape
    nobs_count = measured_gridpoint.shape[1]
    offsets = jnp.array([0, 1, columns, columns + 1], dtype=jnp.int32)
    owner = obs_tile[batch_index, :, 0]
    place = measured_gridpoint[batch_index]
    base = (
        obs_field[batch_index] * (tile_row_count * columns)
        + place // (columns - 1) * columns
        + place % (columns - 1)
    )
    points = (base[:, None] + offsets[None, :]).reshape(-1)
    flat = sample_vectors_prior.reshape(sample_total_size, fields * tile_row_count * columns)
    values = jnp.take(flat, points, axis=1).reshape(sample_total_size, nobs_count, 4)
    local_prior = jnp.sum(values * obs_weights[batch_index][None], axis=-1)
    owned_mask = owner == my_tile
    return (local_prior, owner, owned_mask)


def share_priors(local_prior, owned_mask):
    masked = jnp.where(owned_mask[None], local_prior, jnp.float32(0.0))
    summed = lax.psum(masked, "dom")
    prior = lax.all_gather(summed, "mem", axis=0, tiled=True)
    return prior


def batch_mixing(prior, obs_values, observation_variance, localization, batch_index):
    members = prior.shape[0]
    mean_prior = jnp.mean(prior, axis=0)
    ensemble_spread = prior - mean_prior[None]
    variance = jnp.sum(ensemble_spread * ensemble_spread, axis=0) / (members - 1)
    error = observation_variance[batch_index]
    total = variance + error
    gain = (obs_values[batch_index] - mean_prior)[None] / total[None] - ensemble_spread / (
        jnp.sqrt(total) * (jnp.sqrt(error) + jnp.sqrt(total))
    )[None]
    return jnp.einsum(
        "mo,to,no->tmn",
        ensemble_spread,
        localization[batch_index],
        gain,
        precision=lax.Precision.HIGHEST,
    )[0] / (members - 1)


def apply_update(sample_vectors_prior, mixing):
    sample_total_size, fields, tile_row_count, columns = sample_vectors_prior.shape
    members = sample_total_size * lax.axis_size("mem")
    flat = sample_vectors_prior.reshape(sample_total_size, fields * tile_row_count * columns)
    own_columns = lax.dynamic_slice_in_dim(
        mixing, lax.axis_index("mem") * sample_total_size, sample_total_size, 1
    )
    piece = lax.all_gather(flat, "mem", axis=0, tiled=True)
    product = jnp.dot(
        own_columns.T, piece, precision=lax.Precision.HIGHEST, preferred_element_type=jnp.float32
    )
    member_total = jnp.sum(piece, axis=0)
    average = member_total / members
    updated = flat + product - jnp.sum(own_columns, axis=0)[:, None] * average[None]
    return updated.reshape(sample_total_size, fields, tile_row_count, columns)


def on_device(
    sample_vectors_prior,
    smoothing_number,
    cross_quantity_factor,
    obs_tile,
    measured_gridpoint,
    obs_field,
    obs_weights,
    obs_values,
    observation_variance,
    localization,
):
    my_tile = lax.axis_index("dom")
    for step_index in range(STEPS):
        sample_vectors_prior = predicted_quantity(
            sample_vectors_prior, smoothing_number, cross_quantity_factor
        )
    batch_count = obs_values.shape[0]
    for batch_index in range(batch_count):
        local_prior, owner, owned_mask = local_priors(
            sample_vectors_prior,
            obs_tile,
            measured_gridpoint,
            obs_field,
            obs_weights,
            batch_index,
            my_tile,
        )
        prior = share_priors(local_prior, owned_mask)
        mixing = batch_mixing(prior, obs_values, observation_variance, localization, batch_index)
        sample_vectors_prior = apply_update(sample_vectors_prior, mixing)
    return sample_vectors_prior


def solution(mesh):
    placed = (
        P("mem", None, "dom", None),
        P(None, "dom", None),
        P(),
        P(),
        P(),
        P(),
        P(),
        P(),
        P(),
        P(None, "dom", None),
    )
    return jax.shard_map(
        on_device,
        mesh=mesh,
        in_specs=placed,
        out_specs=P("mem", None, "dom", None),
        check_vma=False,
    )
```

profile of v0, /device:TPU:0, one launch (start us, length us, event | category | flops | bytes accessed | tf_op | source)
XLA Modules:
  0.0 319.6 jit_solution(7989411049781242106)
XLA Ops:
  6.5 1.5 copy.48
  8.1 0.0 copy-start.8
  8.1 0.6 fusion.50
  8.7 1.3 collective-permute-start
  10.0 3.6 %collective-permute-start.1 = (f32[4,5,1,256]{3,1,2,0:T(8,128)}, f32[4,5,1,256]{3,1,2,0:T(8,128)}, u32[]{:S(2)}, u32[]{:S(2)}) collective-permute-start(f32[4,5,1,256]{3,1,2,0:T(8,128)} %get-tuple-element.12), channel_id=1, source_target_pairs={{0,1},{1,2},{2,3},{3,4},{4,5},{5,6},{6,7},{8,9},{9,10},{10,11},{11... | collective-permute-start | bytes 61448 | tf_op jit(solution)/shard_map/ppermute | solution.py:17
  13.6 0.9 broadcast_remainder_fusion
  14.5 0.9 compare_reduce_fusion
  15.4 0.8 slice_multiply_fusion
  16.2 1.3 broadcast_add_fusion
  17.5 0.6 add.178
  18.1 0.6 compare_and_fusion.1
  18.8 0.6 fusion.51
  19.4 0.6 add.189
  20.1 0.1 copy.41
  20.2 1.3 select_maximum_fusion.2
  21.5 0.0 copy-start.12
  21.5 2.3 fusion.4
  23.8 1.3 collective-permute-start.2
  25.1 4.6 %collective-permute-start.3 = (f32[4,5,1,256]{3,1,2,0:T(8,128)S(1)}, f32[4,5,1,256]{3,1,2,0:T(8,128)S(1)}, u32[]{:S(2)}, u32[]{:S(2)}) collective-permute-start(f32[4,5,1,256]{3,1,2,0:T(8,128)S(1)} %get-tuple-element.10), channel_id=1, source_target_pairs={{0,1},{1,2},{2,3},{3,4},{4,5},{5,6},{6,7},{8,9},{9,10},{10,11},{11... | collective-permute-start | bytes 61448 | tf_op jit(solution)/shard_map/ppermute | solution.py:17
  29.7 0.6 compare_reduce_fusion.1
  30.3 0.4 copy.52
  30.7 1.3 copy.56
  32.1 0.5 select_maximum_fusion
  32.6 1.4 fusion.3
  34.0 0.2 copy.50
  34.2 1.2 reshape.217
  35.4 0.4 copy.59
  35.8 0.0 copy-start.6
  35.9 10.0 %copy.51 = f32[4,40960]{0,1:T(8,128)} copy(f32[4,40960]{1,0:T(4,128)S(1)} %bitcast.60) | data formatting | bytes 1310720 | tf_op jit(solution)/shard_map/reshape | solution.py:90
  45.8 0.0 all-gather.7.cloned.1.call-update
  45.9 0.2 all-gather.9.cloned.1.call-start
  46.1 34.7 %gather_fusion = f32[8192,4]{1,0:T(8,128)} fusion(f32[4,40960]{0,1:T(8,128)} %copy.51, s32[8192]{0:T(1024)S(1)} %fusion.31), kind=kCustom, calls=%fused_computation.clone | custom fusion | bytes 294912 | tf_op jit(solution)/shard_map/jit(_take)/gather | solution.py:55
  80.8 6.2 %broadcast_select_fusion.1 = f32[8192,4]{1,0:T(8,128)S(1)} fusion(f32[8192,4]{1,0:T(8,128)} %gather_fusion, pred[8192]{0:T(1024)(128)(4,1)S(1)} %copy-done.10), kind=kLoop, calls=%fused_computation.11 | loop fusion | flops 32768 | bytes 270336 | tf_op jit(solution)/shard_map/jit(_take)/select_n | solution.py:55
  87.0 11.2 %multiply_reduce_fusion.1 = f32[4,2048]{0,1:T(8,128)S(1)} fusion(f32[4,2048,4]{0,2,1:T(4,128)S(1)} %bitcast.56, f32[2048,4]{1,0:T(8,128)S(1)} %copy.52), kind=kLoop, calls=%fused_computation.7 | loop fusion | flops 57344 | bytes 196608 | tf_op jit(solution)/shard_map/reduce_sum | solution.py:56
  98.3 0.0 copy-start.14
  98.3 0.3 broadcast_select_fusion.3
  98.6 58.6 %psum.14 = f32[4,2048]{0,1:T(8,128)S(1)} all-reduce(f32[4,2048]{0,1:T(8,128)S(1)} %broadcast_select_fusion.3), channel_id=1, replica_groups=mesh['mem'=4,'dom'=8] {'dom'}, use_global_device_ids=true, to_apply=%region_1.3 | all-reduce | flops 8192 | bytes 65536 | tf_op jit(solution)/shard_map/psum | solution.py:63
  157.2 0.3 copy.53
  157.5 8.5 %all-gather = f32[4,4,2048]{2,1,0:T(4,128)S(1)} all-gather(f32[1,4,2048]{2,1,0:T(4,128)S(1)} %copy.53), channel_id=1, replica_groups=mesh['mem'=4,'dom'=8] {'mem'}, dimensions={0}, use_global_device_ids=true | all-gather | bytes 163840 | tf_op jit(solution)/shard_map/all_gather | solution.py:64
  166.2 0.1 subtract_divide_fusion.1
  166.3 0.2 fusion.17
  166.5 0.2 fusion.41
  166.7 0.0 all-gather.7.cloned.1.call-done
  166.7 2.5 reduce_sum.94
  169.3 2.0 reshape.218
  171.3 3.4 %fusion.1 = f32[4,40960]{1,0:T(4,128)S(1)} fusion(f32[4,40960]{1,0:T(4,128)} %bitcast.61, f32[16,40960]{1,0:T(8,128)} %reshape.218, f32[40960]{0:T(1024)S(1)} %broadcast_multiply_fusion.1, f32[4]{0:T(128)S(1)} %fusion.41, f32[16,16]{0,1:T(8,128)S(1)} %fusion.17, s32[]{:T(128)S(6)} %select_n.56), kind=kOutput, calls=%fused_computation.5 | convolution fusion | flops 31948864 | bytes 4098564 | tf_op jit(solution)/shard_map/dot_general | solution.py:95
  174.7 10.0 %copy.55 = f32[4,40960]{0,1:T(8,128)} copy(f32[4,40960]{1,0:T(4,128)S(1)} %fusion.1) | data formatting | bytes 1310720 | tf_op jit(solution)/shard_map/sub | solution.py:100
  184.7 0.0 all-gather.9.cloned.1.call-update
  184.7 35.4 %gather_fusion.1 = f32[8192,4]{1,0:T(8,128)} fusion(f32[4,40960]{0,1:T(8,128)} %copy.55, s32[8192]{0:T(1024)S(1)} %fusion.32), kind=kCustom, calls=%fused_computation.1.clone | custom fusion | bytes 294912 | tf_op jit(solution)/shard_map/jit(_take)/gather | solution.py:55
  220.1 6.3 %broadcast_select_fusion = f32[8192,4]{1,0:T(8,128)S(1)} fusion(f32[8192,4]{1,0:T(8,128)} %gather_fusion.1, pred[8192]{0:T(1024)(128)(4,1)S(1)} %compare_and_fusion), kind=kLoop, calls=%fused_computation.10 | loop fusion | flops 32768 | bytes 270336 | tf_op jit(solution)/shard_map/jit(_take)/select_n | solution.py:55
  226.4 11.2 %multiply_reduce_fusion = f32[4,2048]{0,1:T(8,128)S(1)} fusion(f32[4,2048,4]{0,2,1:T(4,128)S(1)} %bitcast.57, f32[2048,4]{1,0:T(8,128)S(1)} %copy-done.7), kind=kLoop, calls=%fused_computation.6 | loop fusion | flops 57344 | bytes 196608 | tf_op jit(solution)/shard_map/reduce_sum | solution.py:56
  237.7 0.3 broadcast_select_fusion.2
  238.0 56.3 %psum.15 = f32[4,2048]{0,1:T(8,128)S(1)} all-reduce(f32[4,2048]{0,1:T(8,128)S(1)} %broadcast_select_fusion.2), channel_id=1, replica_groups=mesh['mem'=4,'dom'=8] {'dom'}, use_global_device_ids=true, to_apply=%region_7.9 | all-reduce | flops 8192 | bytes 65536 | tf_op jit(solution)/shard_map/psum | solution.py:63
  294.3 0.3 copy.57
  294.6 8.7 %all-gather.2 = f32[4,4,2048]{2,1,0:T(4,128)S(1)} all-gather(f32[1,4,2048]{2,1,0:T(4,128)S(1)} %copy.57), channel_id=1, replica_groups=mesh['mem'=4,'dom'=8] {'mem'}, dimensions={0}, use_global_device_ids=true | all-gather | bytes 163840 | tf_op jit(solution)/shard_map/all_gather | solution.py:64
  303.4 0.1 subtract_divide_fusion
  303.5 0.2 fusion.13
  303.8 0.2 fusion.42
  304.0 0.0 all-gather.9.cloned.1.call-done
  304.0 2.5 reduce_sum.99
  306.5 0.0 copy-start.5
  306.6 2.0 reshape.222
  308.6 3.2 %fusion = f32[4,40960]{1,0:T(4,128)S(1)} fusion(f32[4,40960]{1,0:T(4,128)S(1)} %copy-done.5, f32[16,40960]{1,0:T(8,128)} %reshape.222, f32[40960]{0:T(1024)S(1)} %broadcast_multiply_fusion, f32[4]{0:T(128)S(1)} %fusion.42, f32[16,16]{0,1:T(8,128)S(1)} %fusion.13, s32[]{:T(128)S(6)} %select_n.56), kind=kOutput, calls=%fused_computation.3 | convolution fusion | flops 31948864 | bytes 4098564 | tf_op jit(solution)/shard_map/dot_general | solution.py:95
  311.8 1.0 copy.60
  (54 shorter events, 0.4 us)
Async XLA Ops:
  6.5 14.9 %copy-start = (f32[5,5]{1,0:T(8,128)S(1)}, f32[5,5]{1,0:T(8,128)}, u32[]{:S(2)}) copy-start(f32[5,5]{1,0:T(8,128)} %param.16) | copy-start | bytes 304
  6.5 12.2 %copy-start.9 = (f32[2,2048,4]{1,2,0:T(4,128)S(1)}, f32[2,2048,4]{1,2,0:T(4,128)}, u32[]{:S(2)}) copy-start(f32[2,2048,4]{1,2,0:T(4,128)} %param.20) | copy-start | bytes 196612
  6.5 12.2 %copy-start.11 = (f32[2,1,2048]{2,1,0:T(1,128)S(1)}, f32[2,1,2048]{2,1,0:T(1,128)}, u32[]{:S(2)}) copy-start(f32[2,1,2048]{2,1,0:T(1,128)} %param.23) | copy-start | bytes 49156
  6.5 160.2 %all-gather.7.cloned.1.call-start = ((), (), s32[]{:S(2)}) async-start(), calls=%async_computation | async-start | bytes 3276800 | tf_op jit(solution)/shard_map/all_gather | solution.py:94
  8.1 12.0 %copy-start.8 = (f32[5,32,256]{2,1,0:T(8,128)S(1)}, f32[5,32,256]{2,1,0:T(8,128)}, u32[]{:S(2)}) copy-start(f32[5,32,256]{2,1,0:T(8,128)} %param.15) | copy-start | bytes 491524
  8.7 11.5 %collective-permute-start = (f32[4,5,1,256]{3,1,2,0:T(8,128)}, f32[4,5,1,256]{3,1,2,0:T(8,128)}, u32[]{:S(2)}, u32[]{:S(2)}) collective-permute-start(f32[4,5,1,256]{3,1,2,0:T(8,128)} %get-tuple-element.13), channel_id=1, source_target_pairs={{1,0},{2,1},{3,2},{4,3},{5,4},{6,5},{7,6},{9,8},{10,9},{11,10},{12... | collective-permute-start | bytes 61448 | tf_op jit(solution)/shard_map/ppermute | solution.py:19
  10.0 10.2 %collective-permute-start.1 = (f32[4,5,1,256]{3,1,2,0:T(8,128)}, f32[4,5,1,256]{3,1,2,0:T(8,128)}, u32[]{:S(2)}, u32[]{:S(2)}) collective-permute-start(f32[4,5,1,256]{3,1,2,0:T(8,128)} %get-tuple-element.12), channel_id=1, source_target_pairs={{0,1},{1,2},{2,3},{3,4},{4,5},{5,6},{6,7},{8,9},{9,10},{10,11},{11... | collective-permute-start | bytes 61448 | tf_op jit(solution)/shard_map/ppermute | solution.py:17
  21.5 8.2 %copy-start.12 = (s32[2,2048,1]{1,2,0:T(1,128)S(1)}, s32[2,2048,1]{1,2,0:T(1,128)}, u32[]{:S(2)}) copy-start(s32[2,2048,1]{1,2,0:T(1,128)} %param.17) | copy-start | bytes 49156
  23.8 8.3 %collective-permute-start.2 = (f32[4,5,1,256]{3,1,2,0:T(8,128)S(1)}, f32[4,5,1,256]{3,1,2,0:T(8,128)S(1)}, u32[]{:S(2)}, u32[]{:S(2)}) collective-permute-start(f32[4,5,1,256]{3,1,2,0:T(8,128)S(1)} %get-tuple-element.11), channel_id=1, source_target_pairs={{1,0},{2,1},{3,2},{4,3},{5,4},{6,5},{7,6},{9,8},{10,9},{11,10},{12... | collective-permute-start | bytes 61448 | tf_op jit(solution)/shard_map/ppermute | solution.py:19
  25.1 7.0 %collective-permute-start.3 = (f32[4,5,1,256]{3,1,2,0:T(8,128)S(1)}, f32[4,5,1,256]{3,1,2,0:T(8,128)S(1)}, u32[]{:S(2)}, u32[]{:S(2)}) collective-permute-start(f32[4,5,1,256]{3,1,2,0:T(8,128)S(1)} %get-tuple-element.10), channel_id=1, source_target_pairs={{0,1},{1,2},{2,3},{3,4},{4,5},{5,6},{6,7},{8,9},{9,10},{10,11},{11... | collective-permute-start | bytes 61448 | tf_op jit(solution)/shard_map/ppermute | solution.py:17
  35.8 10.0 %copy-start.6 = (f32[1,4,160,256]{3,1,2,0:T(4,128)}, f32[1,4,160,256]{3,1,2,0:T(4,128)S(1)}, u32[]{:S(2)}) copy-start(f32[1,4,160,256]{3,1,2,0:T(4,128)S(1)} %copy.59) | copy-start | bytes 1966084
  35.8 45.0 %copy-start.10 = (pred[8192]{0:T(1024)(128)(4,1)S(1)}, pred[8192]{0:T(1024)(128)(4,1)}, u32[]{:S(2)}) copy-start(pred[8192]{0:T(1024)(128)(4,1)} %compare_and_fusion.1) | copy-start | bytes 24580
  45.9 258.1 %all-gather.9.cloned.1.call-start = ((), (), s32[]{:S(2)}) async-start(), calls=%async_computation.1 | async-start | bytes 3276800 | tf_op jit(solution)/shard_map/all_gather | solution.py:94
  87.0 11.2 %copy-start.15 = (pred[2048]{0:T(1024)(128)(4,1)S(1)}, pred[2048]{0:T(1024)(128)(4,1)}, u32[]{:S(2)}) copy-start(pred[2048]{0:T(1024)(128)(4,1)} %get-tuple-element.7) | copy-start | bytes 6148
  98.3 67.9 %copy-start.13 = (f32[2,2048]{1,0:T(2,128)S(1)}, f32[2,2048]{1,0:T(2,128)}, u32[]{:S(2)}) copy-start(f32[2,2048]{1,0:T(2,128)} %param.21) | copy-start | bytes 49156
  98.3 67.9 %copy-start.14 = (f32[2,2048]{1,0:T(2,128)S(1)}, f32[2,2048]{1,0:T(2,128)}, u32[]{:S(2)}) copy-start(f32[2,2048]{1,0:T(2,128)} %param.22) | copy-start | bytes 49156
  98.3 68.0 %copy-start.17 = (f32[1,1,2048]{2,1,0:T(1,128)S(1)}, f32[1,1,2048]{2,1,0:T(1,128)}, u32[]{:S(2)}) copy-start(f32[1,1,2048]{2,1,0:T(1,128)} %get-tuple-element.21) | copy-start | bytes 24580
  166.7 2.6 copy-start.2
  174.7 10.0 %copy-start.4 = (f32[4,40960]{1,0:T(4,128)}, f32[4,40960]{1,0:T(4,128)S(1)}, u32[]{:S(2)}) copy-start(f32[4,40960]{1,0:T(4,128)S(1)} %fusion.1) | copy-start | bytes 1966084
  220.1 6.3 %copy-start.7 = (f32[2048,4]{1,0:T(8,128)S(1)}, f32[2048,4]{1,0:T(8,128)}, u32[]{:S(2)}) copy-start(f32[2048,4]{1,0:T(8,128)} %copy.56) | copy-start | bytes 98308
  237.7 65.9 %copy-start.16 = (f32[1,1,2048]{2,1,0:T(1,128)S(1)}, f32[1,1,2048]{2,1,0:T(1,128)}, u32[]{:S(2)}) copy-start(f32[1,1,2048]{2,1,0:T(1,128)} %get-tuple-element.20) | copy-start | bytes 24580
  304.0 2.6 copy-start.3
  306.5 2.0 copy-start.5
  306.6 6.2 %copy-start.1 = (f32[5,5]{1,0:T(8,128)S(1)}, f32[5,5]{1,0:T(8,128)}, u32[]{:S(2)}) copy-start(f32[5,5]{1,0:T(8,128)} %param.16) | copy-start | bytes 304
Sparse Core Ops, SparseCore 0:
  46.0 41.8 all-gather.6
  184.9 36.8 all-gather.8
where the time goes:
time: 321 us; the launch traced here: 320 us
  blocking collectives  132 us (41%)
  local copies, waits for them, and re-layouts  104 us (32%)
  other arithmetic  48.2 us (15%)
  between operations  13.9 us (4%)
  starting transfers between devices  11 us (3%)
  matrix products  10.8 us (3%)
    psum x2, blocking collectives, share_priors(): summed = lax.psum(masked, 'dom')  115 us
    gather x2, local copies, waits for them, and re-layouts, local_priors(): jnp.take(flat, points, axis=1).reshape(sample_total_size, nobs_count, 4)  70.1 us
    reduce_sum x2, other arithmetic, local_priors(): local_prior = jnp.sum(values * obs_weights[batch_index][None], axis=-1)  22.4 us
    all_gather x2, blocking collectives, share_priors(): prior = lax.all_gather(summed, 'mem', axis=0, tiled=True)  17.1 us
    select_n x2, other arithmetic, local_priors(): jnp.take(flat, points, axis=1).reshape(sample_total_size, nobs_count, 4)  12.5 us
    sub x1, local copies, waits for them, and re-layouts, apply_update(): flat + product - jnp.sum(own_columns, axis=0)[:, None] * average[None]  10 us
    reshape x1, local copies, waits for them, and re-layouts, apply_update(): sample_vectors_prior.reshape(sample_total_size, fields * tile_row_count *...  9.99 us
    unnamed x47, local copies, waits for them, and re-layouts  9.06 us
  transfers between devices with their start and end apart: 6, of which 0 were waited for; matrix products, arithmetic and copies ran while one was open for 36% of the time, Pallas kernels for 0%

commit v1 on v0

v1 whole, which is shorter than its diff:
```python
import functools

import jax
import jax.numpy as jnp
from jax import lax
from jax.experimental import pallas as pl
from jax.experimental.pallas import tpu as pltpu
from jax.sharding import PartitionSpec as P

STEPS = 2
HALO = 8
MESH = pl.DeviceIdType.MESH
HIGHEST = lax.Precision.HIGHEST
F32 = jnp.float32
BF16 = jnp.bfloat16


def three_parts(a):
    high = a.astype(BF16).astype(F32)
    rest = a - high
    middle = rest.astype(BF16).astype(F32)
    return jnp.concatenate([high, middle, rest - middle], axis=0).astype(BF16)


def iota(shape, dim):
    return lax.broadcasted_iota(jnp.int32, shape, dim)


def kernel(
    nmem, ndom, cap,
    x_ref, s_ref, c_ref, tile_ref, attr_ref, loc_ref,
    out_ref,
    pad, spad, xu, xh, xl, pick, comp, csel, rsel, lbuf, lrow, lcomp,
    pbuf, xg, og, og_in, ps, rb, wb,
    local_sem, halo_send, halo_recv, loc_send, loc_recv, pri_send, pri_recv,
    st_send, st_recv, mix_send, mix_recv, fin_send, fin_recv,
):
    me = lax.axis_index("mem")
    tile = lax.axis_index("dom")
    own, fields, rows, cols = x_ref.shape
    members = own * nmem
    batches, _, nobs = attr_ref.shape
    wide = xu.shape[-1]
    across = cols // wide
    lane_blocks = nobs // 128
    last = ndom - 1

    load_x = pltpu.make_async_copy(x_ref, pad.at[:, :, HALO:HALO + rows, :], local_sem.at[0])
    load_s = pltpu.make_async_copy(s_ref, spad.at[:, HALO:HALO + rows, :], local_sem.at[1])
    load_x.start()
    load_s.start()

    barrier = pltpu.get_barrier_semaphore()
    for d in range(1, nmem):
        pl.semaphore_signal(barrier, inc=1, device_id={"mem": lax.rem(me + d, nmem)}, device_id_type=MESH)
    for d in range(1, ndom):
        pl.semaphore_signal(barrier, inc=1, device_id={"dom": lax.rem(tile + d, ndom)}, device_id_type=MESH)

    @pl.when(tile == 0)
    def _():
        pad[:, :, 0:HALO, :] = jnp.zeros((own, fields, HALO, cols), F32)
        spad[:, 0:HALO, :] = jnp.zeros((fields, HALO, cols), F32)

    @pl.when(tile == last)
    def _():
        pad[:, :, HALO + rows:, :] = jnp.zeros((own, fields, HALO, cols), F32)
        spad[:, HALO + rows:, :] = jnp.zeros((fields, HALO, cols), F32)

    pl.semaphore_wait(barrier, nmem + ndom - 2)

    def halo(src, dst, to, slot):
        return pltpu.make_async_remote_copy(
            src_ref=src, dst_ref=dst, send_sem=halo_send.at[slot], recv_sem=halo_recv.at[slot],
            device_id={"dom": to}, device_id_type=MESH,
        )

    below = lax.rem(tile + ndom - 1, ndom)
    above = lax.rem(tile + 1, ndom)
    down = [
        halo(x_ref.at[:, :, 0:HALO, :], pad.at[:, :, HALO + rows:HALO + rows + HALO, :], below, 0),
        halo(s_ref.at[:, 0:HALO, :], spad.at[:, HALO + rows:HALO + rows + HALO, :], below, 1),
    ]
    up = [
        halo(x_ref.at[:, :, rows - HALO:rows, :], pad.at[:, :, 0:HALO, :], above, 2),
        halo(s_ref.at[:, rows - HALO:rows, :], spad.at[:, 0:HALO, :], above, 3),
    ]

    @pl.when(tile > 0)
    def _():
        for copy in down:
            copy.start()

    @pl.when(tile < last)
    def _():
        for copy in up:
            copy.start()

    loc_copies = []
    for d in range(1, ndom):
        copy = pltpu.make_async_remote_copy(
            src_ref=loc_ref, dst_ref=lbuf.at[tile], send_sem=loc_send.at[d], recv_sem=loc_recv.at[d],
            device_id={"dom": lax.rem(tile + d, ndom)}, device_id_type=MESH,
        )
        copy.start()
        loc_copies.append(copy)
    lbuf[tile] = loc_ref[...]

    count = batches * lane_blocks
    owned = tile_ref[...] == tile
    ownf = jnp.where(owned, 1.0, 0.0).astype(F32)
    ahead = jnp.where(iota((128, 128), 0) < iota((128, 128), 1), 1.0, 0.0).astype(BF16)
    row_i, row_j = iota((count, count), 0), iota((count, count), 1)
    prior_rows = jnp.where((row_j < row_i) & (row_j // lane_blocks == row_i // lane_blocks), 1.0, 0.0).astype(BF16)
    within = jnp.dot(ownf.astype(BF16), ahead, preferred_element_type=F32)
    offset = jnp.sum(jnp.dot(prior_rows, ownf.astype(BF16), preferred_element_type=F32), axis=1, keepdims=True)
    rank = jnp.where(owned, within + offset, -1.0)
    rank = jnp.concatenate([rank, jnp.full((128 - count, 128), -1.0, F32)], axis=0) if count < 128 else rank
    rank_t = jnp.transpose(rank)
    slots = iota((128, cap), 1).astype(F32)
    for b in range(batches):
        for k in range(lane_blocks):
            at = b * lane_blocks + k
            pick[b, k * 128:(k + 1) * 128, :] = jnp.where(rank_t[:, at:at + 1] == slots, 1.0, 0.0).astype(BF16)
    for b in range(batches):
        got = jnp.dot(three_parts(attr_ref[b]), pick[b], preferred_element_type=F32)
        packed = got[0:8] + got[8:16] + got[16:24]
        comp[b] = packed
        column = packed[1:2, :].astype(jnp.int32)
        line = packed[0:1, :].astype(jnp.int32)
        col_at = iota((cols, cap), 0)
        csel[b, 0] = jnp.where(col_at == column, 1.0, 0.0).astype(BF16)
        csel[b, 1] = jnp.where(col_at == column + 1, 1.0, 0.0).astype(BF16)
        line_at = iota((fields * rows, cap), 0)
        here, after = line_at == line, line_at == line + 1
        rsel[b, 0] = jnp.where(here, packed[2:3, :], jnp.where(after, packed[4:5, :], 0.0))
        rsel[b, 1] = jnp.where(here, packed[3:4, :], jnp.where(after, packed[5:6, :], 0.0))

    load_x.wait()
    load_s.wait()

    @pl.when(tile > 0)
    def _():
        for copy in up:
            copy.wait_recv()

    @pl.when(tile < last)
    def _():
        for copy in down:
            copy.wait_recv()

    height = rows + 2 * HALO
    lane = iota((height, cols), 1)

    def member(m, carry):
        x = [pad[m, f] for f in range(fields)]
        for _ in range(STEPS):
            new = []
            for f in range(fields):
                v = x[f]
                lap = pltpu.roll(v, 1, 0) + pltpu.roll(v, height - 1, 0)
                lap = lap + jnp.where(lane < cols - 1, pltpu.roll(v, cols - 1, 1), 0.0)
                lap = lap + jnp.where(lane > 0, pltpu.roll(v, 1, 1), 0.0) - 4.0 * v
                mixed = c_ref[f, 0] * x[0]
                for g in range(1, fields):
                    mixed = mixed + c_ref[f, g] * x[g]
                new.append(v + spad[f] * lap + mixed)
            x = new
        for f in range(fields):
            v = x[f][HALO:HALO + rows]
            high = v.astype(BF16)
            xh[m, f * rows:(f + 1) * rows, :] = high
            xl[m, f * rows:(f + 1) * rows, :] = (v - high.astype(F32)).astype(BF16)
            for k in range(nmem):
                r, c = k // across * 8, k % across * wide
                xu[k, m, f] = v[r:r + 8, c:c + wide]
        return carry

    lax.fori_loop(0, own, member, 0)

    def observe(m, carry):
        for b in range(batches):
            total = jnp.zeros((1, cap), F32)
            for side in range(2):
                t = jnp.dot(xh[m], csel[b, side], preferred_element_type=F32)
                t = t + jnp.dot(xl[m], csel[b, side], preferred_element_type=F32)
                total = total + jnp.sum(t * rsel[b, side], axis=0, keepdims=True)
            pbuf[me, m, :, b * cap:(b + 1) * cap] = total
        return carry

    lax.fori_loop(0, own, observe, 0)
    pri_copies = []
    for d in range(1, nmem):
        copy = pltpu.make_async_remote_copy(
            src_ref=pbuf.at[me], dst_ref=pbuf.at[me], send_sem=pri_send.at[d], recv_sem=pri_recv.at[d],
            device_id={"mem": lax.rem(me + d, nmem)}, device_id_type=MESH,
        )
        copy.start()
        pri_copies.append(copy)
    st_copies = []
    for d in range(1, nmem):
        to = lax.rem(me + d, nmem)
        copy = pltpu.make_async_remote_copy(
            src_ref=xu.at[to], dst_ref=xg.at[me], send_sem=st_send.at[d], recv_sem=st_recv.at[d],
            device_id={"mem": to}, device_id_type=MESH,
        )
        copy.start()
        st_copies.append(copy)
    xg[me] = xu[me]

    for copy in loc_copies:
        copy.wait_recv()
    for t in range(ndom):
        lrow[t:t + 1, :] = lbuf[t]
    for b in range(batches):
        got = jnp.dot(
            three_parts(lrow[:, b * nobs:(b + 1) * nobs]), pick[b], preferred_element_type=F32
        )
        lcomp[b] = got[0:ndom] + got[ndom:2 * ndom] + got[2 * ndom:3 * ndom]

    for copy in pri_copies:
        copy.wait_recv()

    def gather_prior(b):
        return jnp.concatenate(
            [pbuf[i, m, :, b * cap:(b + 1) * cap] for i in range(nmem) for m in range(own)], axis=0
        )

    def mixing_of(b, prior):
        value = comp[b, 6:7, :]
        error = comp[b, 7:8, :]
        error = jnp.where(error > 0.0, error, 1.0)
        mean = jnp.sum(prior, axis=0, keepdims=True) / members
        spread = prior - mean
        total = jnp.sum(spread * spread, axis=0, keepdims=True) / (members - 1) + error
        root = jnp.sqrt(total)
        gain = (value - mean) / total - spread / (root * (jnp.sqrt(error) + root))
        local = jnp.concatenate([gain * lcomp[b, t:t + 1, :] for t in range(ndom)], axis=0)
        wide_spread = jnp.concatenate([spread, jnp.zeros((128 - members, cap), F32)], axis=0)
        part = lax.dot_general(
            local, wide_spread, (((1,), (1,)), ((), ())), precision=HIGHEST, preferred_element_type=F32
        ) / (members - 1)
        for t in range(ndom):
            ps[b, t] = part[t * members:(t + 1) * members]
        copies = []
        for d in range(1, ndom):
            to = lax.rem(tile + d, ndom)
            copy = pltpu.make_async_remote_copy(
                src_ref=ps.at[b, to], dst_ref=rb.at[b, tile],
                send_sem=mix_send.at[b, d], recv_sem=mix_recv.at[b, d],
                device_id={"dom": to}, device_id_type=MESH,
            )
            copy.start()
            copies.append(copy)
        rb[b, tile] = ps[b, tile]
        for copy in copies:
            copy.wait_recv()
        return jnp.sum(rb[b], axis=0)[:, 0:members], copies

    eye = jnp.where(iota((members, members), 0) == iota((members, members), 1), 1.0, 0.0).astype(F32)
    mix_copies = []
    advance = eye
    folded = jnp.zeros((members, members), F32)
    for b in range(batches):
        prior = gather_prior(b)
        if b > 0:
            anomaly = prior - jnp.sum(prior, axis=0, keepdims=True) / members
            prior = prior + jnp.dot(folded, anomaly, precision=HIGHEST, preferred_element_type=F32)
        mix, copies = mixing_of(b, prior)
        mix_copies += copies
        folded = folded + (
            mix if b == 0 else jnp.dot(mix, advance, precision=HIGHEST, preferred_element_type=F32)
        )
        advance = eye + folded - jnp.sum(folded, axis=0, keepdims=True) / members
    weight = eye + folded - jnp.sum(folded, axis=1, keepdims=True) / members

    pairs = members * members
    choose = jnp.where(iota((pairs, members), 0) // members == iota((pairs, members), 1), 1.0, 0.0).astype(F32)
    spreadw = jnp.dot(choose, weight, precision=HIGHEST, preferred_element_type=F32)
    spreadw = jnp.where(iota((pairs, members), 0) % members == iota((pairs, members), 1), spreadw, 0.0)
    wb[...] = jnp.broadcast_to(jnp.sum(spreadw, axis=1, keepdims=True), (pairs, wide)).reshape(members, members, wide)

    for copy in st_copies:
        copy.wait_recv()

    def apply(to, dst):
        def one(i, carry):
            w = wb[to * own + i]
            acc = [jnp.zeros((8, wide), F32)] * fields
            for m in range(members):
                scale = jnp.broadcast_to(w[m:m + 1, :], (8, wide))
                for f in range(fields):
                    acc[f] = acc[f] + scale * xg[m // own, m % own, f]
            for f in range(fields):
                dst[to if dst is og else me, i, f] = acc[f]
            return carry

        lax.fori_loop(0, own, one, 0)

    fin_copies = []
    for d in range(1, nmem):
        to = lax.rem(me + d, nmem)
        apply(to, og)
        copy = pltpu.make_async_remote_copy(
            src_ref=og.at[to], dst_ref=og_in.at[me], send_sem=fin_send.at[d], recv_sem=fin_recv.at[d],
            device_id={"mem": to}, device_id_type=MESH,
        )
        copy.start()
        fin_copies.append(copy)
    apply(me, og_in)
    for copy in fin_copies:
        copy.wait_recv()
    for k in range(nmem):
        r, c = k // across * 8, k % across * wide
        out_ref[:, :, r:r + 8, c:c + wide] = og_in[k]

    @pl.when(tile > 0)
    def _():
        for copy in down:
            copy.wait_send()

    @pl.when(tile < last)
    def _():
        for copy in up:
            copy.wait_send()

    for copy in loc_copies + pri_copies + st_copies + mix_copies + fin_copies:
        copy.wait_send()


def on_device(nmem, ndom, x, smooth, cross, obs_tile, place, field, obs_weights, values, variance, localization):
    own, fields, rows, cols = x.shape
    batches, nobs = place.shape
    cap = 2 * nobs // ndom
    members = own * nmem
    wide = rows * cols // (8 * nmem)
    line = field * rows + place // (cols - 1)
    column = place % (cols - 1)
    attrs = jnp.concatenate(
        [
            line[:, None].astype(F32),
            column[:, None].astype(F32),
            jnp.transpose(obs_weights, (0, 2, 1)),
            values[:, None],
            variance[:, None],
        ],
        axis=1,
    )
    vmem = pl.BlockSpec(memory_space=pltpu.VMEM)
    anywhere = pl.BlockSpec(memory_space=pl.ANY)
    dma = pltpu.SemaphoreType.DMA
    return pl.pallas_call(
        functools.partial(kernel, nmem, ndom, cap),
        out_shape=jax.ShapeDtypeStruct(x.shape, F32),
        in_specs=[anywhere, anywhere, pl.BlockSpec(memory_space=pltpu.SMEM), vmem, vmem, vmem],
        out_specs=vmem,
        scratch_shapes=[
            pltpu.VMEM((own, fields, rows + 2 * HALO, cols), F32),
            pltpu.VMEM((fields, rows + 2 * HALO, cols), F32),
            pltpu.VMEM((nmem, own, fields, 8, wide), F32),
            pltpu.VMEM((own, fields * rows, cols), BF16),
            pltpu.VMEM((own, fields * rows, cols), BF16),
            pltpu.VMEM((batches, nobs, cap), BF16),
            pltpu.VMEM((batches, 8, cap), F32),
            pltpu.VMEM((batches, 2, cols, cap), BF16),
            pltpu.VMEM((batches, 2, fields * rows, cap), F32),
            pltpu.VMEM((ndom, 1, batches * nobs), F32),
            pltpu.VMEM((ndom, batches * nobs), F32),
            pltpu.VMEM((batches, ndom, cap), F32),
            pltpu.VMEM((nmem, own, 1, batches * cap), F32),
            pltpu.VMEM((nmem, own, fields, 8, wide), F32),
            pltpu.VMEM((nmem, own, fields, 8, wide), F32),
            pltpu.VMEM((nmem, own, fields, 8, wide), F32),
            pltpu.VMEM((batches, ndom, members, 128), F32),
            pltpu.VMEM((batches, ndom, members, 128), F32),
            pltpu.VMEM((members, members, wide), F32),
            dma((2,)), dma((4,)), dma((4,)),
            dma((ndom,)), dma((ndom,)),
            dma((nmem,)), dma((nmem,)),
            dma((nmem,)), dma((nmem,)),
            dma((batches, ndom)), dma((batches, ndom)),
            dma((nmem,)), dma((nmem,)),
        ],
        compiler_params=pltpu.CompilerParams(
            collective_id=0, has_side_effects=True, vmem_limit_bytes=48 * 1024 * 1024
        ),
    )(
        x,
        smooth,
        cross,
        obs_tile.reshape(batches * nobs // 128, 128),
        attrs,
        localization.reshape(1, batches * nobs),
    )


def solution(mesh):
    placed = (
        P("mem", None, "dom", None),
        P(None, "dom", None),
        P(),
        P(),
        P(),
        P(),
        P(),
        P(),
        P(),
        P(None, "dom", None),
    )
    return jax.shard_map(
        functools.partial(on_device, mesh.shape["mem"], mesh.shape["dom"]),
        mesh=mesh,
        in_specs=placed,
        out_specs=P("mem", None, "dom", None),
        check_vma=False,
    )
```

time: 321 us -> 43.4 us (0.14)
  blocking collectives: 132 us -> 0 us
  local copies, waits for them, and re-layouts: 104 us -> 4.87 us
  other arithmetic: 48.2 us -> 0.08 us
  Pallas kernels: 0 us -> 37.8 us
  between operations: 13.9 us -> 0.08 us
  starting transfers between devices: 11 us -> 0 us
  matrix products: 10.8 us -> 0 us
    psum x2 -> x0, blocking collectives: 115 us -> none  [share_priors(): summed = lax.psum(masked, 'dom')]
    gather x2 -> x0, local copies, waits for them, and re-layouts: 70.1 us -> none  [local_priors(): jnp.take(flat, points, axis=1).reshape(sample_total_size, nobs_count, 4)]
    pallas_call x0 -> x1, Pallas kernels: none -> 37.8 us  [on_device(): pl.pallas_call(functools.partial(kernel, nmem, ndom, cap), out_shape=jax....]
    reduce_sum x10 -> x0, other arithmetic: 28 us -> none  [the longest x2 22.4 us: local_priors(): local_prior = jnp.sum(values * obs_weights[batch_index][None], axis=-1)]
    all_gather x2 -> x0, blocking collectives: 17.1 us -> none  [share_priors(): prior = lax.all_gather(summed, 'mem', axis=0, tiled=True)]
    select_n x4 -> x0, other arithmetic: 13.2 us -> none  [the longest x2 12.5 us: local_priors(): jnp.take(flat, points, axis=1).reshape(sample_total_size, nobs_count, 4)]
    ppermute x4 -> x0, starting transfers between devices: 10.8 us -> none  [the longest x2 8.22 us: with_halo(): lax.ppermute(tail, axis, [(i, (i + 1) % count) for i in range(ends)])]
    dot_general x6 -> x0, matrix products: 10.8 us -> none  [the longest x2 6.59 us: apply_update(): jnp.dot(own_columns.T, piece, precision=lax.Precision.HIGHEST, preferred_...]
  transfers between devices with their start and end apart: 6 -> 0, of which waited for: 0 -> 0; matrix products, arithmetic and copies ran while one was open for 36% -> 0% of each run, Pallas kernels for 0% -> 0%
where the time goes in v1:
time: 43.4 us; the launch traced here: 42.9 us
  Pallas kernels  37.8 us (87%)
  local copies, waits for them, and re-layouts  4.87 us (11%)
    pallas_call x1, Pallas kernels, on_device(): pl.pallas_call(functools.partial(kernel, nmem, ndom, cap), out_shape=jax....  37.8 us
    unnamed x19, local copies, waits for them, and re-layouts  3.96 us

profile of v1, /device:TPU:0, one launch (start us, length us, event | category | flops | bytes accessed | tf_op | source)
XLA Modules:
  0.0 42.9 jit_solution(4940280933676702205)
XLA Ops:
  0.0 0.0 copy-start.6
  0.0 0.7 %broadcast_in_dim.8 = f32[2,1,2048]{2,1,0:T(1,128)S(1)} reshape(f32[2,2048]{1,0:T(2,128)} %param.17) | data formatting | bytes 32768 | tf_op jit(solution)/shard_map/broadcast_in_dim | solution.py:343
  0.7 0.0 copy-done.6
  0.8 0.0 copy-start.7
  0.8 0.0 copy-start.8
  0.8 0.7 %copy-done.7 = s32[2,2048]{1,0:T(2,128)S(1)} copy-done((s32[2,2048]{1,0:T(2,128)S(1)}, s32[2,2048]{1,0:T(2,128)}, u32[]{:S(2)}) %copy-start.7) | copy-done | bytes 16408
  1.5 0.0 copy-done.8
  1.5 0.0 copy-start.5
  1.5 0.1 fusion
  1.6 0.0 copy-start.1
  1.6 0.7 %copy-done.5 = f32[2,2048,4]{1,2,0:T(4,128)S(1)} copy-done((f32[2,2048,4]{1,2,0:T(4,128)S(1)}, f32[2,2048,4]{1,2,0:T(4,128)}, u32[]{:S(2)}) %copy-start.5) | copy-done | bytes 65560
  2.3 0.0 copy-start.2
  2.3 0.0 copy-start.3
  2.3 0.0 copy-start.4
  2.3 0.1 concatenate.3.attr_ref
  2.5 0.0 copy-done.1
  2.5 0.6 %copy-done.2 = s32[2,2048,1]{1,2,0:T(1,128)S(1)} copy-done((s32[2,2048,1]{1,2,0:T(1,128)S(1)}, s32[2,2048,1]{1,2,0:T(1,128)}, u32[]{:S(2)}) %copy-start.2) | copy-done | bytes 16408
  3.1 0.0 copy-done.3
  3.1 0.0 copy-done.4
  3.1 0.0 copy-start
  3.1 1.1 %copy-done = f32[4,5,32,256]{3,2,1,0:T(8,128)S(1)} copy-done((f32[4,5,32,256]{3,2,1,0:T(8,128)S(1)}, f32[4,5,32,256]{3,2,1,0:T(8,128)}, u32[]{:S(2)}) %copy-start) | copy-done | bytes 655384
  4.2 37.8 %shard_map.100 = f32[4,5,32,256]{3,2,1,0:T(8,128)S(1)} custom-call(f32[4,5,32,256]{3,2,1,0:T(8,128)S(1)} %copy-done, f32[5,32,256]{2,1,0:T(8,128)S(1)} %copy-done.1, f32[5,5]{1,0:T(8,128)S(1)} %copy-done.4, s32[32,128]{1,0:T(8,128)S(1)} %bitcast.5, f32[2,8,2048]{2,1,0:T(8,128)S(1)} %concatenate.3.attr_ref, f32[1,4096]{1,0:T(1,128)S(1)} %bitcast.6), custom_call_target="tpu_custom_call" | custom-call | tf_op jit(solution)/shard_map/pallas_call | solution.py:351
  42.0 0.8 %copy.13 = f32[4,5,32,256]{3,2,1,0:T(8,128)} copy(f32[4,5,32,256]{3,2,1,0:T(8,128)S(1)} %shard_map.100) | data formatting | bytes 1310720
  (3 shorter events, 0.0 us)
Async XLA Ops:
  0.0 0.7 %copy-start.6 = (f32[2,2048]{1,0:T(2,128)S(1)}, f32[2,2048]{1,0:T(2,128)}, u32[]{:S(2)}) copy-start(f32[2,2048]{1,0:T(2,128)} %param.18) | copy-start | bytes 49156
  0.8 0.7 %copy-start.7 = (s32[2,2048]{1,0:T(2,128)S(1)}, s32[2,2048]{1,0:T(2,128)}, u32[]{:S(2)}) copy-start(s32[2,2048]{1,0:T(2,128)} %param.14) | copy-start | bytes 49156
  0.8 0.7 %copy-start.8 = (s32[2,2048]{1,0:T(2,128)S(1)}, s32[2,2048]{1,0:T(2,128)}, u32[]{:S(2)}) copy-start(s32[2,2048]{1,0:T(2,128)} %param.15) | copy-start | bytes 49156
  1.5 0.8 %copy-start.5 = (f32[2,2048,4]{1,2,0:T(4,128)S(1)}, f32[2,2048,4]{1,2,0:T(4,128)}, u32[]{:S(2)}) copy-start(f32[2,2048,4]{1,2,0:T(4,128)} %param.16) | copy-start | bytes 196612
  1.6 0.9 %copy-start.1 = (f32[5,32,256]{2,1,0:T(8,128)S(1)}, f32[5,32,256]{2,1,0:T(8,128)}, u32[]{:S(2)}) copy-start(f32[5,32,256]{2,1,0:T(8,128)} %s_ref.1) | copy-start | bytes 491524
  2.3 0.7 %copy-start.2 = (s32[2,2048,1]{1,2,0:T(1,128)S(1)}, s32[2,2048,1]{1,2,0:T(1,128)}, u32[]{:S(2)}) copy-start(s32[2,2048,1]{1,2,0:T(1,128)} %param.13) | copy-start | bytes 49156
  2.3 0.8 %copy-start.3 = (f32[2,1,2048]{2,1,0:T(1,128)S(1)}, f32[2,1,2048]{2,1,0:T(1,128)}, u32[]{:S(2)}) copy-start(f32[2,1,2048]{2,1,0:T(1,128)} %param.19) | copy-start | bytes 49156
  2.3 0.8 %copy-start.4 = (f32[5,5]{1,0:T(8,128)S(1)}, f32[5,5]{1,0:T(8,128)}, u32[]{:S(2)}) copy-start(f32[5,5]{1,0:T(8,128)} %c_ref.1) | copy-start | bytes 304
  3.1 1.1 %copy-start = (f32[4,5,32,256]{3,2,1,0:T(8,128)S(1)}, f32[4,5,32,256]{3,2,1,0:T(8,128)}, u32[]{:S(2)}) copy-start(f32[4,5,32,256]{3,2,1,0:T(8,128)} %x_ref.1) | copy-start | bytes 1966084

commit v2 on v1

--- a/solution.py
+++ b/solution.py
@@ -9,6 +9,7 @@
 
 STEPS = 2
 HALO = 8
+GATHERED = 1
 MESH = pl.DeviceIdType.MESH
 HIGHEST = lax.Precision.HIGHEST
 F32 = jnp.float32
@@ -22,15 +23,30 @@
     return jnp.concatenate([high, middle, rest - middle], axis=0).astype(BF16)
 
 
+def two_parts(a):
+    high = a.astype(BF16)
+    return high, (a - high.astype(F32)).astype(BF16)
+
+
+def partner(index, distance, count):
+    to, step = 0, 1
+    while step < count:
+        bit = lax.rem(index // step, 2)
+        to = to + step * (1 - bit if distance // step % 2 else bit)
+        step *= 2
+    return to
+
+
 def iota(shape, dim):
     return lax.broadcasted_iota(jnp.int32, shape, dim)
 
 
 def kernel(
     nmem, ndom, cap,
-    x_ref, s_ref, c_ref, tile_ref, attr_ref, loc_ref,
+    x_ref, s_ref, c_ref, tile_hbm, place_hbm, field_hbm, weight_hbm, value_hbm, var_hbm, loc_hbm,
     out_ref,
-    pad, spad, xu, xh, xl, pick, comp, csel, rsel, lbuf, lrow, lcomp,
+    tile_ref, place_ref, field_ref, weight_ref, value_ref, var_ref, loc_ref,
+    pad, spad, xs, xall, xu, xh, xl, pick, comp, csel, rsel, lbuf, lrow, lcomp,
     pbuf, xg, og, og_in, ps, rb, wb,
     local_sem, halo_send, halo_recv, loc_send, loc_recv, pri_send, pri_recv,
     st_send, st_recv, mix_send, mix_recv, fin_send, fin_recv,
@@ -39,7 +55,10 @@
     tile = lax.axis_index("dom")
     own, fields, rows, cols = x_ref.shape
     members = own * nmem
-    batches, _, nobs = attr_ref.shape
+    batches, nobs = place_ref.shape
+    gathered = xs.shape[1]
+    rest = fields - gathered
+    groups = members // 8
     wide = xu.shape[-1]
     across = cols // wide
     lane_blocks = nobs // 128
@@ -47,6 +66,15 @@
 
     load_x = pltpu.make_async_copy(x_ref, pad.at[:, :, HALO:HALO + rows, :], local_sem.at[0])
     load_s = pltpu.make_async_copy(s_ref, spad.at[:, HALO:HALO + rows, :], local_sem.at[1])
+    loads = [
+        pltpu.make_async_copy(src, dst, local_sem.at[2 + i])
+        for i, (src, dst) in enumerate([
+            (tile_hbm, tile_ref), (place_hbm, place_ref), (field_hbm, field_ref), (weight_hbm, weight_ref),
+            (value_hbm, value_ref), (var_hbm, var_ref), (loc_hbm, loc_ref),
+        ])
+    ]
+    for copy in loads:
+        copy.start()
     load_x.start()
     load_s.start()
 
@@ -66,44 +94,8 @@
         pad[:, :, HALO + rows:, :] = jnp.zeros((own, fields, HALO, cols), F32)
         spad[:, HALO + rows:, :] = jnp.zeros((fields, HALO, cols), F32)
 
-    pl.semaphore_wait(barrier, nmem + ndom - 2)
-
-    def halo(src, dst, to, slot):
-        return pltpu.make_async_remote_copy(
-            src_ref=src, dst_ref=dst, send_sem=halo_send.at[slot], recv_sem=halo_recv.at[slot],
-            device_id={"dom": to}, device_id_type=MESH,
-        )
-
-    below = lax.rem(tile + ndom - 1, ndom)
-    above = lax.rem(tile + 1, ndom)
-    down = [
-        halo(x_ref.at[:, :, 0:HALO, :], pad.at[:, :, HALO + rows:HALO + rows + HALO, :], below, 0),
-        halo(s_ref.at[:, 0:HALO, :], spad.at[:, HALO + rows:HALO + rows + HALO, :], below, 1),
-    ]
-    up = [
-        halo(x_ref.at[:, :, rows - HALO:rows, :], pad.at[:, :, 0:HALO, :], above, 2),
-        halo(s_ref.at[:, rows - HALO:rows, :], spad.at[:, 0:HALO, :], above, 3),
-    ]
-
-    @pl.when(tile > 0)
-    def _():
-        for copy in down:
-            copy.start()
-
-    @pl.when(tile < last)
-    def _():
-        for copy in up:
-            copy.start()
-
-    loc_copies = []
-    for d in range(1, ndom):
-        copy = pltpu.make_async_remote_copy(
-            src_ref=loc_ref, dst_ref=lbuf.at[tile], send_sem=loc_send.at[d], recv_sem=loc_recv.at[d],
-            device_id={"dom": lax.rem(tile + d, ndom)}, device_id_type=MESH,
-        )
-        copy.start()
-        loc_copies.append(copy)
-    lbuf[tile] = loc_ref[...]
+    for copy in loads:
+        copy.wait()
 
     count = batches * lane_blocks
     owned = tile_ref[...] == tile
@@ -121,8 +113,51 @@
         for k in range(lane_blocks):
             at = b * lane_blocks + k
             pick[b, k * 128:(k + 1) * 128, :] = jnp.where(rank_t[:, at:at + 1] == slots, 1.0, 0.0).astype(BF16)
+
+    pl.semaphore_wait(barrier, nmem + ndom - 2)
+
+    def halo(src, dst, to, slot):
+        return pltpu.make_async_remote_copy(
+            src_ref=src, dst_ref=dst, send_sem=halo_send.at[slot], recv_sem=halo_recv.at[slot],
+            device_id={"dom": to}, device_id_type=MESH,
+        )
+
+    below = lax.rem(tile + ndom - 1, ndom)
+    above = lax.rem(tile + 1, ndom)
+    down = [
+        halo(x_ref.at[:, :, 0:HALO, :], pad.at[:, :, HALO + rows:HALO + rows + HALO, :], below, 0),
+        halo(s_ref.at[:, 0:HALO, :], spad.at[:, HALO + rows:HALO + rows + HALO, :], below, 1),
+    ]
+    up = [
+        halo(x_ref.at[:, :, rows - HALO:rows, :], pad.at[:, :, 0:HALO, :], above, 2),
+        halo(s_ref.at[:, rows - HALO:rows, :], spad.at[:, 0:HALO, :], above, 3),
+    ]
+
+    @pl.when(tile > 0)
+    def _():
+        for copy in down:
+            copy.start()
+
+    @pl.when(tile < last)
+    def _():
+        for copy in up:
+            copy.start()
+
+
     for b in range(batches):
-        got = jnp.dot(three_parts(attr_ref[b]), pick[b], preferred_element_type=F32)
+        place = place_ref[b:b + 1, :].astype(F32)
+        row = jnp.floor((place + 0.5) * (1.0 / (cols - 1)))
+        attrs = jnp.concatenate(
+            [
+                field_ref[b:b + 1, :].astype(F32) * rows + row,
+                place - row * (cols - 1),
+                weight_ref[b],
+                value_ref[b:b + 1, :],
+                var_ref[b:b + 1, :],
+            ],
+            axis=0,
+        )
+        got = jnp.dot(three_parts(attrs), pick[b], preferred_element_type=F32)
         packed = got[0:8] + got[8:16] + got[16:24]
         comp[b] = packed
         column = packed[1:2, :].astype(jnp.int32)
@@ -147,6 +182,16 @@
     def _():
         for copy in down:
             copy.wait_recv()
+
+    loc_copies = []
+    for d in range(ndom - 1, 0, -1):
+        copy = pltpu.make_async_remote_copy(
+            src_ref=loc_ref, dst_ref=lbuf.at[tile], send_sem=loc_send.at[d], recv_sem=loc_recv.at[d],
+            device_id={"dom": partner(tile, d, ndom)}, device_id_type=MESH,
+        )
+        copy.start()
+        loc_copies.append(copy)
+    lbuf[tile] = loc_ref[...]
 
     height = rows + 2 * HALO
     lane = iota((height, cols), 1)
@@ -167,44 +212,47 @@
             x = new
         for f in range(fields):
             v = x[f][HALO:HALO + rows]
-            high = v.astype(BF16)
-            xh[m, f * rows:(f + 1) * rows, :] = high
-            xl[m, f * rows:(f + 1) * rows, :] = (v - high.astype(F32)).astype(BF16)
-            for k in range(nmem):
-                r, c = k // across * 8, k % across * wide
-                xu[k, m, f] = v[r:r + 8, c:c + wide]
+            xh[m, f * rows:(f + 1) * rows, :], xl[m, f * rows:(f + 1) * rows, :] = two_parts(v)
+            if f < gathered:
+                xs[m, f] = v
+            else:
+                for k in range(nmem):
+                    r, c = k // across * 8, k % across * wide
+                    xu[k, m, f - gathered] = v[r:r + 8, c:c + wide]
         return carry
 
     lax.fori_loop(0, own, member, 0)
 
-    def observe(m, carry):
-        for b in range(batches):
-            total = jnp.zeros((1, cap), F32)
-            for side in range(2):
-                t = jnp.dot(xh[m], csel[b, side], preferred_element_type=F32)
-                t = t + jnp.dot(xl[m], csel[b, side], preferred_element_type=F32)
-                total = total + jnp.sum(t * rsel[b, side], axis=0, keepdims=True)
-            pbuf[me, m, :, b * cap:(b + 1) * cap] = total
-        return carry
-
-    lax.fori_loop(0, own, observe, 0)
+    high = xh[...].reshape(own * fields * rows, cols)
+    low = xl[...].reshape(own * fields * rows, cols)
+    for b in range(batches):
+        total = 0.0
+        for side in range(2):
+            t = jnp.dot(high, csel[b, side], preferred_element_type=F32)
+            t = t + jnp.dot(low, csel[b, side], preferred_element_type=F32)
+            total = total + jnp.sum(t.reshape(own, fields * rows, cap) * rsel[b, side], axis=1)
+        for m in range(own):
+            pbuf[me, m, :, b * cap:(b + 1) * cap] = total[m:m + 1]
+
     pri_copies = []
-    for d in range(1, nmem):
+    for d in range(nmem - 1, 0, -1):
         copy = pltpu.make_async_remote_copy(
             src_ref=pbuf.at[me], dst_ref=pbuf.at[me], send_sem=pri_send.at[d], recv_sem=pri_recv.at[d],
-            device_id={"mem": lax.rem(me + d, nmem)}, device_id_type=MESH,
+            device_id={"mem": partner(me, d, nmem)}, device_id_type=MESH,
         )
         copy.start()
         pri_copies.append(copy)
     st_copies = []
-    for d in range(1, nmem):
-        to = lax.rem(me + d, nmem)
-        copy = pltpu.make_async_remote_copy(
-            src_ref=xu.at[to], dst_ref=xg.at[me], send_sem=st_send.at[d], recv_sem=st_recv.at[d],
-            device_id={"mem": to}, device_id_type=MESH,
-        )
-        copy.start()
-        st_copies.append(copy)
+    for d in range(nmem - 1, 0, -1):
+        to = partner(me, d, nmem)
+        for slot, (src, dst) in enumerate([(xu.at[to], xg.at[me]), (xs, xall.at[me])]):
+            copy = pltpu.make_async_remote_copy(
+                src_ref=src, dst_ref=dst, send_sem=st_send.at[slot, d], recv_sem=st_recv.at[slot, d],
+                device_id={"mem": to}, device_id_type=MESH,
+            )
+            copy.start()
+            st_copies.append(copy)
+    xall[me] = xs[...]
     xg[me] = xu[me]
 
     for copy in loc_copies:
@@ -234,16 +282,27 @@
         total = jnp.sum(spread * spread, axis=0, keepdims=True) / (members - 1) + error
         root = jnp.sqrt(total)
         gain = (value - mean) / total - spread / (root * (jnp.sqrt(error) + root))
-        local = jnp.concatenate([gain * lcomp[b, t:t + 1, :] for t in range(ndom)], axis=0)
-        wide_spread = jnp.concatenate([spread, jnp.zeros((128 - members, cap), F32)], axis=0)
+        left, right = [], []
+        for g in range(groups):
+            local = jnp.concatenate(
+                [gain[8 * g:8 * g + 8] * lcomp[b, t:t + 1, :] for t in range(ndom)], axis=0
+            )
+            placed = [jnp.zeros((g * members, cap), F32)] if g else []
+            placed += [spread / (members - 1)]
+            placed += [jnp.zeros((128 - (g + 1) * members, cap), F32)] if (g + 1) * members < 128 else []
+            local_high, local_low = two_parts(local)
+            placed_high, placed_low = two_parts(jnp.concatenate(placed, axis=0))
+            left += [local_high, local_high, local_low]
+            right += [placed_high, placed_low, placed_high]
         part = lax.dot_general(
-            local, wide_spread, (((1,), (1,)), ((), ())), precision=HIGHEST, preferred_element_type=F32
-        ) / (members - 1)
+            jnp.concatenate(left, axis=1), jnp.concatenate(right, axis=1), (((1,), (1,)), ((), ())),
+            preferred_element_type=F32,
+        )
         for t in range(ndom):
-            ps[b, t] = part[t * members:(t + 1) * members]
+            ps[b, t] = part[8 * t:8 * t + 8]
         copies = []
-        for d in range(1, ndom):
-            to = lax.rem(tile + d, ndom)
+        for d in range(ndom - 1, 0, -1):
+            to = partner(tile, d, ndom)
             copy = pltpu.make_async_remote_copy(
                 src_ref=ps.at[b, to], dst_ref=rb.at[b, tile],
                 send_sem=mix_send.at[b, d], recv_sem=mix_recv.at[b, d],
@@ -254,7 +313,8 @@
         rb[b, tile] = ps[b, tile]
         for copy in copies:
             copy.wait_recv()
-        return jnp.sum(rb[b], axis=0)[:, 0:members], copies
+        got = jnp.sum(rb[b], axis=0)
+        return jnp.concatenate([got[:, g * members:(g + 1) * members] for g in range(groups)], axis=0), copies
 
     eye = jnp.where(iota((members, members), 0) == iota((members, members), 1), 1.0, 0.0).astype(F32)
     mix_copies = []
@@ -277,7 +337,7 @@
     choose = jnp.where(iota((pairs, members), 0) // members == iota((pairs, members), 1), 1.0, 0.0).astype(F32)
     spreadw = jnp.dot(choose, weight, precision=HIGHEST, preferred_element_type=F32)
     spreadw = jnp.where(iota((pairs, members), 0) % members == iota((pairs, members), 1), spreadw, 0.0)
-    wb[...] = jnp.broadcast_to(jnp.sum(spreadw, axis=1, keepdims=True), (pairs, wide)).reshape(members, members, wide)
+    wb[...] = jnp.broadcast_to(jnp.sum(spreadw, axis=1, keepdims=True), (pairs, cols)).reshape(members, members, cols)
 
     for copy in st_copies:
         copy.wait_recv()
@@ -285,20 +345,20 @@
     def apply(to, dst):
         def one(i, carry):
             w = wb[to * own + i]
-            acc = [jnp.zeros((8, wide), F32)] * fields
+            acc = [jnp.zeros((8, wide), F32)] * rest
             for m in range(members):
-                scale = jnp.broadcast_to(w[m:m + 1, :], (8, wide))
-                for f in range(fields):
+                scale = jnp.broadcast_to(w[m:m + 1, 0:wide], (8, wide))
+                for f in range(rest):
                     acc[f] = acc[f] + scale * xg[m // own, m % own, f]
-            for f in range(fields):
+            for f in range(rest):
                 dst[to if dst is og else me, i, f] = acc[f]
             return carry
 
         lax.fori_loop(0, own, one, 0)
 
     fin_copies = []
-    for d in range(1, nmem):
-        to = lax.rem(me + d, nmem)
+    for d in range(nmem - 1, 0, -1):
+        to = partner(me, d, nmem)
         apply(to, og)
         copy = pltpu.make_async_remote_copy(
             src_ref=og.at[to], dst_ref=og_in.at[me], send_sem=fin_send.at[d], recv_sem=fin_recv.at[d],
@@ -307,11 +367,22 @@
         copy.start()
         fin_copies.append(copy)
     apply(me, og_in)
+
+    def apply_gathered(i, carry):
+        w = wb[me * own + i]
+        for f in range(gathered):
+            acc = jnp.zeros((rows, cols), F32)
+            for m in range(members):
+                acc = acc + jnp.broadcast_to(w[m:m + 1, :], (rows, cols)) * xall[m // own, m % own, f]
+            out_ref[i, f] = acc
+        return carry
+
+    lax.fori_loop(0, own, apply_gathered, 0)
     for copy in fin_copies:
         copy.wait_recv()
     for k in range(nmem):
         r, c = k // across * 8, k % across * wide
-        out_ref[:, :, r:r + 8, c:c + wide] = og_in[k]
+        out_ref[:, gathered:, r:r + 8, c:c + wide] = og_in[k]
 
     @pl.when(tile > 0)
     def _():
@@ -333,30 +404,28 @@
     cap = 2 * nobs // ndom
     members = own * nmem
     wide = rows * cols // (8 * nmem)
-    line = field * rows + place // (cols - 1)
-    column = place % (cols - 1)
-    attrs = jnp.concatenate(
-        [
-            line[:, None].astype(F32),
-            column[:, None].astype(F32),
-            jnp.transpose(obs_weights, (0, 2, 1)),
-            values[:, None],
-            variance[:, None],
-        ],
-        axis=1,
-    )
+    rest = fields - GATHERED
     vmem = pl.BlockSpec(memory_space=pltpu.VMEM)
     anywhere = pl.BlockSpec(memory_space=pl.ANY)
     dma = pltpu.SemaphoreType.DMA
     return pl.pallas_call(
         functools.partial(kernel, nmem, ndom, cap),
         out_shape=jax.ShapeDtypeStruct(x.shape, F32),
-        in_specs=[anywhere, anywhere, pl.BlockSpec(memory_space=pltpu.SMEM), vmem, vmem, vmem],
+        in_specs=[anywhere, anywhere, pl.BlockSpec(memory_space=pltpu.SMEM)] + [anywhere] * 7,
         out_specs=vmem,
         scratch_shapes=[
+            pltpu.VMEM((batches * nobs // 128, 128), jnp.int32),
+            pltpu.VMEM((batches, nobs), jnp.int32),
+            pltpu.VMEM((batches, nobs), jnp.int32),
+            pltpu.VMEM((batches, 4, nobs), F32),
+            pltpu.VMEM((batches, nobs), F32),
+            pltpu.VMEM((batches, nobs), F32),
+            pltpu.VMEM((1, batches * nobs), F32),
             pltpu.VMEM((own, fields, rows + 2 * HALO, cols), F32),
             pltpu.VMEM((fields, rows + 2 * HALO, cols), F32),
-            pltpu.VMEM((nmem, own, fields, 8, wide), F32),
+            pltpu.VMEM((own, GATHERED, rows, cols), F32),
+            pltpu.VMEM((nmem, own, GATHERED, rows, cols), F32),
+            pltpu.VMEM((nmem, own, rest, 8, wide), F32),
             pltpu.VMEM((own, fields * rows, cols), BF16),
             pltpu.VMEM((own, fields * rows, cols), BF16),
             pltpu.VMEM((batches, nobs, cap), BF16),
@@ -367,28 +436,32 @@
             pltpu.VMEM((ndom, batches * nobs), F32),
             pltpu.VMEM((batches, ndom, cap), F32),
             pltpu.VMEM((nmem, own, 1, batches * cap), F32),
-            pltpu.VMEM((nmem, own, fields, 8, wide), F32),
-            pltpu.VMEM((nmem, own, fields, 8, wide), F32),
-            pltpu.VMEM((nmem, own, fields, 8, wide), F32),
-            pltpu.VMEM((batches, ndom, members, 128), F32),
-            pltpu.VMEM((batches, ndom, members, 128), F32),
-            pltpu.VMEM((members, members, wide), F32),
-            dma((2,)), dma((4,)), dma((4,)),
+            pltpu.VMEM((nmem, own, rest, 8, wide), F32),
+            pltpu.VMEM((nmem, own, rest, 8, wide), F32),
+            pltpu.VMEM((nmem, own, rest, 8, wide), F32),
+            pltpu.VMEM((batches, ndom, 8, 128), F32),
+            pltpu.VMEM((batches, ndom, 8, 128), F32),
+            pltpu.VMEM((members, members, cols), F32),
+            dma((9,)), dma((4,)), dma((4,)),
             dma((ndom,)), dma((ndom,)),
             dma((nmem,)), dma((nmem,)),
-            dma((nmem,)), dma((nmem,)),
+            dma((2, nmem)), dma((2, nmem)),
             dma((batches, ndom)), dma((batches, ndom)),
             dma((nmem,)), dma((nmem,)),
         ],
         compiler_params=pltpu.CompilerParams(
-            collective_id=0, has_side_effects=True, vmem_limit_bytes=48 * 1024 * 1024
+            collective_id=0, has_side_effects=True, vmem_limit_bytes=60 * 1024 * 1024
         ),
     )(
         x,
         smooth,
         cross,
         obs_tile.reshape(batches * nobs // 128, 128),
-        attrs,
+        place,
+        field,
+        jnp.transpose(obs_weights, (0, 2, 1)),
+        values,
+        variance,
         localization.reshape(1, batches * nobs),
     )
 

time: 43.4 us -> 43.2 us (level)
  Pallas kernels: 37.8 us -> 40.9 us
  local copies, waits for them, and re-layouts: 4.87 us -> 1.99 us
    pallas_call x1, Pallas kernels: 37.8 us -> 40.9 us  [on_device(): pl.pallas_call(functools.partial(kernel, nmem, ndom, cap), out_shape=jax....]
    unnamed x19 -> x1, local copies, waits for them, and re-layouts: 3.96 us -> 1.99 us
    broadcast_in_dim x2 -> x0, local copies, waits for them, and re-layouts: 0.76 us -> none  [the longest x1 0.74 us: on_device(): values[:, None]]
where the time goes in v2:
time: 43.2 us; the launch traced here: 42.9 us
  Pallas kernels  40.9 us (95%)
  local copies, waits for them, and re-layouts  1.99 us (5%)
    pallas_call x1, Pallas kernels, on_device(): pl.pallas_call(functools.partial(kernel, nmem, ndom, cap), out_shape=jax....  40.9 us
    unnamed x1, local copies, waits for them, and re-layouts  1.99 us

profile of v2, /device:TPU:0, one launch (start us, length us, event | category | flops | bytes accessed | tf_op | source)
XLA Modules:
  0.0 42.9 jit_solution(8572617381711011079)
XLA Ops:
  0.0 40.9 %shard_map.100 = f32[4,5,32,256]{3,2,1,0:T(8,128)} custom-call(f32[4,5,32,256]{3,2,1,0:T(8,128)} %x_ref.1, f32[5,32,256]{2,1,0:T(8,128)} %s_ref.1, f32[5,5]{1,0:T(8,128)} %c_ref.1, s32[32,128]{1,0:T(8,128)} %bitcast.4, s32[2,2048]{1,0:T(2,128)} %place_hbm.1, s32[2,2048]{1,0:T(2,128)} %field_hbm.1, f32[2,4,2048]{2,1,0:T(4,128)} %bitcast.3, ...), custom_call_target="tpu_custom_call" | custom-call | tf_op jit(solution)/shard_map/pallas_call | solution.py:411
  40.9 2.0 %copy.12 = f32[4,5,32,256]{3,2,1,0:T(8,128)} copy(f32[4,5,32,256]{3,2,1,0:T(8,128)} %shard_map.100) | data formatting | bytes 1310720

commit v3 on v2

--- a/solution.py
+++ b/solution.py
@@ -94,6 +94,36 @@
         pad[:, :, HALO + rows:, :] = jnp.zeros((own, fields, HALO, cols), F32)
         spad[:, HALO + rows:, :] = jnp.zeros((fields, HALO, cols), F32)
 
+    pl.semaphore_wait(barrier, nmem + ndom - 2)
+
+    def halo(src, dst, to, slot):
+        return pltpu.make_async_remote_copy(
+            src_ref=src, dst_ref=dst, send_sem=halo_send.at[slot], recv_sem=halo_recv.at[slot],
+            device_id={"dom": to}, device_id_type=MESH,
+        )
+
+    below = lax.rem(tile + ndom - 1, ndom)
+    above = lax.rem(tile + 1, ndom)
+    down = [
+        halo(x_ref.at[:, :, 0:HALO, :], pad.at[:, :, HALO + rows:HALO + rows + HALO, :], below, 0),
+        halo(s_ref.at[:, 0:HALO, :], spad.at[:, HALO + rows:HALO + rows + HALO, :], below, 1),
+    ]
+    up = [
+        halo(x_ref.at[:, :, rows - HALO:rows, :], pad.at[:, :, 0:HALO, :], above, 2),
+        halo(s_ref.at[:, rows - HALO:rows, :], spad.at[:, 0:HALO, :], above, 3),
+    ]
+
+    @pl.when(tile > 0)
+    def _():
+        for copy in down:
+            copy.start()
+
+    @pl.when(tile < last)
+    def _():
+        for copy in up:
+            copy.start()
+
+
     for copy in loads:
         copy.wait()
 
@@ -109,42 +139,11 @@
     rank = jnp.concatenate([rank, jnp.full((128 - count, 128), -1.0, F32)], axis=0) if count < 128 else rank
     rank_t = jnp.transpose(rank)
     slots = iota((128, cap), 1).astype(F32)
-    for b in range(batches):
+
+    def prepare(b):
         for k in range(lane_blocks):
             at = b * lane_blocks + k
             pick[b, k * 128:(k + 1) * 128, :] = jnp.where(rank_t[:, at:at + 1] == slots, 1.0, 0.0).astype(BF16)
-
-    pl.semaphore_wait(barrier, nmem + ndom - 2)
-
-    def halo(src, dst, to, slot):
-        return pltpu.make_async_remote_copy(
-            src_ref=src, dst_ref=dst, send_sem=halo_send.at[slot], recv_sem=halo_recv.at[slot],
-            device_id={"dom": to}, device_id_type=MESH,
-        )
-
-    below = lax.rem(tile + ndom - 1, ndom)
-    above = lax.rem(tile + 1, ndom)
-    down = [
-        halo(x_ref.at[:, :, 0:HALO, :], pad.at[:, :, HALO + rows:HALO + rows + HALO, :], below, 0),
-        halo(s_ref.at[:, 0:HALO, :], spad.at[:, HALO + rows:HALO + rows + HALO, :], below, 1),
-    ]
-    up = [
-        halo(x_ref.at[:, :, rows - HALO:rows, :], pad.at[:, :, 0:HALO, :], above, 2),
-        halo(s_ref.at[:, rows - HALO:rows, :], spad.at[:, 0:HALO, :], above, 3),
-    ]
-
-    @pl.when(tile > 0)
-    def _():
-        for copy in down:
-            copy.start()
-
-    @pl.when(tile < last)
-    def _():
-        for copy in up:
-            copy.start()
-
-
-    for b in range(batches):
         place = place_ref[b:b + 1, :].astype(F32)
         row = jnp.floor((place + 0.5) * (1.0 / (cols - 1)))
         attrs = jnp.concatenate(
@@ -169,6 +168,8 @@
         here, after = line_at == line, line_at == line + 1
         rsel[b, 0] = jnp.where(here, packed[2:3, :], jnp.where(after, packed[4:5, :], 0.0))
         rsel[b, 1] = jnp.where(here, packed[3:4, :], jnp.where(after, packed[5:6, :], 0.0))
+
+    prepare(0)
 
     load_x.wait()
     load_s.wait()
@@ -223,55 +224,62 @@
 
     lax.fori_loop(0, own, member, 0)
 
-    high = xh[...].reshape(own * fields * rows, cols)
-    low = xl[...].reshape(own * fields * rows, cols)
-    for b in range(batches):
+    pri_copies, st_copies = [], []
+
+    def observe(b):
+        high = xh[...].reshape(own * fields * rows, cols)
+        low = xl[...].reshape(own * fields * rows, cols)
         total = 0.0
         for side in range(2):
             t = jnp.dot(high, csel[b, side], preferred_element_type=F32)
             t = t + jnp.dot(low, csel[b, side], preferred_element_type=F32)
             total = total + jnp.sum(t.reshape(own, fields * rows, cap) * rsel[b, side], axis=1)
         for m in range(own):
-            pbuf[me, m, :, b * cap:(b + 1) * cap] = total[m:m + 1]
-
-    pri_copies = []
-    for d in range(nmem - 1, 0, -1):
-        copy = pltpu.make_async_remote_copy(
-            src_ref=pbuf.at[me], dst_ref=pbuf.at[me], send_sem=pri_send.at[d], recv_sem=pri_recv.at[d],
-            device_id={"mem": partner(me, d, nmem)}, device_id_type=MESH,
-        )
-        copy.start()
-        pri_copies.append(copy)
-    st_copies = []
-    for d in range(nmem - 1, 0, -1):
-        to = partner(me, d, nmem)
-        for slot, (src, dst) in enumerate([(xu.at[to], xg.at[me]), (xs, xall.at[me])]):
+            pbuf[b, me, m] = total[m:m + 1]
+        copies = []
+        for d in range(nmem - 1, 0, -1):
+            copy = pltpu.make_async_remote_copy(
+                src_ref=pbuf.at[b, me], dst_ref=pbuf.at[b, me],
+                send_sem=pri_send.at[b, d], recv_sem=pri_recv.at[b, d],
+                device_id={"mem": partner(me, d, nmem)}, device_id_type=MESH,
+            )
+            copy.start()
+            copies.append(copy)
+        pri_copies.append(copies)
+
+    def send_states(slot):
+        for d in range(nmem - 1, 0, -1):
+            to = partner(me, d, nmem)
+            src, dst = [(xu.at[to], xg.at[me]), (xs, xall.at[me])][slot]
             copy = pltpu.make_async_remote_copy(
                 src_ref=src, dst_ref=dst, send_sem=st_send.at[slot, d], recv_sem=st_recv.at[slot, d],
                 device_id={"mem": to}, device_id_type=MESH,
             )
             copy.start()
             st_copies.append(copy)
-    xall[me] = xs[...]
+
+    def localize(b):
+        got = jnp.dot(
+            three_parts(lrow[:, b * nobs:(b + 1) * nobs]), pick[b], preferred_element_type=F32
+        )
+        lcomp[b] = got[0:ndom] + got[ndom:2 * ndom] + got[2 * ndom:3 * ndom]
+
+    def gather_prior(b):
+        for copy in pri_copies[b]:
+            copy.wait_recv()
+        return jnp.concatenate([pbuf[b, i, m] for i in range(nmem) for m in range(own)], axis=0)
+
+    observe(0)
+    send_states(0)
     xg[me] = xu[me]
 
     for copy in loc_copies:
         copy.wait_recv()
     for t in range(ndom):
         lrow[t:t + 1, :] = lbuf[t]
-    for b in range(batches):
-        got = jnp.dot(
-            three_parts(lrow[:, b * nobs:(b + 1) * nobs]), pick[b], preferred_element_type=F32
-        )
-        lcomp[b] = got[0:ndom] + got[ndom:2 * ndom] + got[2 * ndom:3 * ndom]
-
-    for copy in pri_copies:
-        copy.wait_recv()
-
-    def gather_prior(b):
-        return jnp.concatenate(
-            [pbuf[i, m, :, b * cap:(b + 1) * cap] for i in range(nmem) for m in range(own)], axis=0
-        )
+    localize(0)
+    for b in range(1, batches):
+        prepare(b)
 
     def mixing_of(b, prior):
         value = comp[b, 6:7, :]
@@ -311,10 +319,13 @@
             copy.start()
             copies.append(copy)
         rb[b, tile] = ps[b, tile]
+        return copies
+
+    def received(b, copies):
         for copy in copies:
             copy.wait_recv()
         got = jnp.sum(rb[b], axis=0)
-        return jnp.concatenate([got[:, g * members:(g + 1) * members] for g in range(groups)], axis=0), copies
+        return jnp.concatenate([got[:, g * members:(g + 1) * members] for g in range(groups)], axis=0)
 
     eye = jnp.where(iota((members, members), 0) == iota((members, members), 1), 1.0, 0.0).astype(F32)
     mix_copies = []
@@ -325,8 +336,16 @@
         if b > 0:
             anomaly = prior - jnp.sum(prior, axis=0, keepdims=True) / members
             prior = prior + jnp.dot(folded, anomaly, precision=HIGHEST, preferred_element_type=F32)
-        mix, copies = mixing_of(b, prior)
+        copies = mixing_of(b, prior)
         mix_copies += copies
+        if b == 0:
+            for later in range(1, batches):
+                observe(later)
+            send_states(1)
+            xall[me] = xs[...]
+            for later in range(1, batches):
+                localize(later)
+        mix = received(b, copies)
         folded = folded + (
             mix if b == 0 else jnp.dot(mix, advance, precision=HIGHEST, preferred_element_type=F32)
         )
@@ -339,7 +358,7 @@
     spreadw = jnp.where(iota((pairs, members), 0) % members == iota((pairs, members), 1), spreadw, 0.0)
     wb[...] = jnp.broadcast_to(jnp.sum(spreadw, axis=1, keepdims=True), (pairs, cols)).reshape(members, members, cols)
 
-    for copy in st_copies:
+    for copy in st_copies[0:nmem - 1]:
         copy.wait_recv()
 
     def apply(to, dst):
@@ -368,6 +387,9 @@
         fin_copies.append(copy)
     apply(me, og_in)
 
+    for copy in st_copies[nmem - 1:]:
+        copy.wait_recv()
+
     def apply_gathered(i, carry):
         w = wb[me * own + i]
         for f in range(gathered):
@@ -394,7 +416,7 @@
         for copy in up:
             copy.wait_send()
 
-    for copy in loc_copies + pri_copies + st_copies + mix_copies + fin_copies:
+    for copy in loc_copies + sum(pri_copies, []) + st_copies + mix_copies + fin_copies:
         copy.wait_send()
 
 
@@ -406,7 +428,7 @@
     wide = rows * cols // (8 * nmem)
     rest = fields - GATHERED
     vmem = pl.BlockSpec(memory_space=pltpu.VMEM)
-    anywhere = pl.BlockSpec(memory_space=pl.ANY)
+    anywhere = pl.BlockSpec(memory_space=pltpu.HBM)
     dma = pltpu.SemaphoreType.DMA
     return pl.pallas_call(
         functools.partial(kernel, nmem, ndom, cap),
@@ -435,7 +457,7 @@
             pltpu.VMEM((ndom, 1, batches * nobs), F32),
             pltpu.VMEM((ndom, batches * nobs), F32),
             pltpu.VMEM((batches, ndom, cap), F32),
-            pltpu.VMEM((nmem, own, 1, batches * cap), F32),
+            pltpu.VMEM((batches, nmem, own, 1, cap), F32),
             pltpu.VMEM((nmem, own, rest, 8, wide), F32),
             pltpu.VMEM((nmem, own, rest, 8, wide), F32),
             pltpu.VMEM((nmem, own, rest, 8, wide), F32),
@@ -444,7 +466,7 @@
             pltpu.VMEM((members, members, cols), F32),
             dma((9,)), dma((4,)), dma((4,)),
             dma((ndom,)), dma((ndom,)),
-            dma((nmem,)), dma((nmem,)),
+            dma((batches, nmem)), dma((batches, nmem)),
             dma((2, nmem)), dma((2, nmem)),
             dma((batches, ndom)), dma((batches, ndom)),
             dma((nmem,)), dma((nmem,)),

time: 43.2 us -> 41.2 us (0.954)
  Pallas kernels: 40.9 us -> 39 us
    pallas_call x1, Pallas kernels: 40.9 us -> 39 us  [on_device(): pl.pallas_call(functools.partial(kernel, nmem, ndom, cap), out_shape=jax....]
where the time goes in v3:
time: 41.2 us; the launch traced here: 41 us
  Pallas kernels  39 us (95%)
  local copies, waits for them, and re-layouts  1.99 us (5%)
    pallas_call x1, Pallas kernels, on_device(): pl.pallas_call(functools.partial(kernel, nmem, ndom, cap), out_shape=jax....  39 us
    unnamed x1, local copies, waits for them, and re-layouts  1.99 us

profile of v3, /device:TPU:0, one launch (start us, length us, event | category | flops | bytes accessed | tf_op | source)
XLA Modules:
  0.0 41.0 jit_solution(607617332266757640)
XLA Ops:
  0.0 39.0 %shard_map.100 = f32[4,5,32,256]{3,2,1,0:T(8,128)} custom-call(f32[4,5,32,256]{3,2,1,0:T(8,128)} %x_ref.1, f32[5,32,256]{2,1,0:T(8,128)} %s_ref.1, f32[5,5]{1,0:T(8,128)} %c_ref.1, s32[32,128]{1,0:T(8,128)} %bitcast.4, s32[2,2048]{1,0:T(2,128)} %place_hbm.1, s32[2,2048]{1,0:T(2,128)} %field_hbm.1, f32[2,4,2048]{2,1,0:T(4,128)} %bitcast.3, ...), custom_call_target="tpu_custom_call" | custom-call | tf_op jit(solution)/shard_map/pallas_call | solution.py:433
  39.0 2.0 %copy.12 = f32[4,5,32,256]{3,2,1,0:T(8,128)} copy(f32[4,5,32,256]{3,2,1,0:T(8,128)} %shard_map.100) | data formatting | bytes 1310720

commit v4 on v3

--- a/solution.py
+++ b/solution.py
@@ -396,15 +396,16 @@
             acc = jnp.zeros((rows, cols), F32)
             for m in range(members):
                 acc = acc + jnp.broadcast_to(w[m:m + 1, :], (rows, cols)) * xall[m // own, m % own, f]
-            out_ref[i, f] = acc
+            for r in range(rows // 8):
+                out_ref[r, i, f] = acc[8 * r:8 * r + 8]
         return carry
 
     lax.fori_loop(0, own, apply_gathered, 0)
     for copy in fin_copies:
         copy.wait_recv()
     for k in range(nmem):
-        r, c = k // across * 8, k % across * wide
-        out_ref[:, gathered:, r:r + 8, c:c + wide] = og_in[k]
+        c = k % across * wide
+        out_ref[k // across, :, gathered:, :, c:c + wide] = og_in[k]
 
     @pl.when(tile > 0)
     def _():
@@ -430,9 +431,9 @@
     vmem = pl.BlockSpec(memory_space=pltpu.VMEM)
     anywhere = pl.BlockSpec(memory_space=pltpu.HBM)
     dma = pltpu.SemaphoreType.DMA
-    return pl.pallas_call(
+    bands = pl.pallas_call(
         functools.partial(kernel, nmem, ndom, cap),
-        out_shape=jax.ShapeDtypeStruct(x.shape, F32),
+        out_shape=jax.ShapeDtypeStruct((rows // 8, own, fields, 8, cols), F32),
         in_specs=[anywhere, anywhere, pl.BlockSpec(memory_space=pltpu.SMEM)] + [anywhere] * 7,
         out_specs=vmem,
         scratch_shapes=[
@@ -486,6 +487,7 @@
         variance,
         localization.reshape(1, batches * nobs),
     )
+    return jnp.transpose(bands, (1, 2, 0, 3, 4)).reshape(own, fields, rows, cols)
 
 
 def solution(mesh):

time: 41.2 us -> 41.2 us (level)
    reshape x0 -> x1, local copies, waits for them, and re-layouts: none -> 2 us  [on_device(): jnp.transpose(bands, (1, 2, 0, 3, 4)).reshape(own, fields, rows, cols)]
    unnamed x1 -> x0, local copies, waits for them, and re-layouts: 1.99 us -> none
where the time goes in v4:
time: 41.2 us; the launch traced here: 41 us
  Pallas kernels  39 us (95%)
  local copies, waits for them, and re-layouts  2 us (5%)
    pallas_call x1, Pallas kernels, on_device(): pl.pallas_call(functools.partial(kernel, nmem, ndom, cap), out_shape=jax....  39 us
    reshape x1, local copies, waits for them, and re-layouts, on_device(): jnp.transpose(bands, (1, 2, 0, 3, 4)).reshape(own, fields, rows, cols)  2 us

profile of v4, /device:TPU:0, one launch (start us, length us, event | category | flops | bytes accessed | tf_op | source)
XLA Modules:
  0.0 41.0 jit_solution(11424523327220831349)
XLA Ops:
  0.0 39.0 %shard_map.100 = f32[4,4,5,8,256]{4,3,2,1,0:T(8,128)} custom-call(f32[4,5,32,256]{3,2,1,0:T(8,128)} %x_ref.1, f32[5,32,256]{2,1,0:T(8,128)} %s_ref.1, f32[5,5]{1,0:T(8,128)} %c_ref.1, s32[32,128]{1,0:T(8,128)} %bitcast.9, s32[2,2048]{1,0:T(2,128)} %place_hbm.1, s32[2,2048]{1,0:T(2,128)} %field_hbm.1, f32[2,4,2048]{2,1,0:T(4,128)} %bitcast.8, ...), custom_call_target="tpu_custom_call" | custom-call | tf_op jit(solution)/shard_map/pallas_call | solution.py:434
  39.0 2.0 %copy_bitcast_fusion = f32[4,5,32,256]{3,2,1,0:T(8,128)} fusion(f32[4,4,5,8,256]{4,3,2,1,0:T(8,128)} %shard_map.100), kind=kLoop, calls=%fused_computation | loop fusion | bytes 1310720 | tf_op jit(solution)/shard_map/reshape | solution.py:490
